TPU v7x, 512 devices: a whole 4x8x8 slice. The times are simulated.
512 devices in a mesh: tm: 8 (over y), pts: 64 (over x, z, core).
Axes of the slice: x: 4, y: 8, z: 8, core: 2. Of those that a mesh axis runs over, the one named last changes fastest.
Arguments:
- precip: float32 [2048, 65536], P('tm', 'pts'), may hold values from -150 to 300, as said below
- thresholds: float32 [64], replicated, may hold values from -1 to 5
- bin_index: int32 [65536], P('pts'), may hold values from 0 to 63
- test_matrix: float32 [2048, 256], P('tm'), may hold values from -0.125 to 0.125
Outputs:
- basis: float32 [65536, 256], P(('pts', 'tm'))
- factor: float32 [256, 256], replicated
Inputs may be any that keep to these rules, and one draw needn't show every extreme that they name: `precip`: precipitation records.
All inputs are finite; a program needn't handle non-finite values.
Results may differ from a plain program's by a relative error of at most 0.0003.
Values sent between devices are 32-bit elements; how exact they have to be, the bound alone decides.
A program may use at most 64 MiB of HBM per device.

v0:
```python
import math

import jax
import jax.numpy as jnp
from jax import lax
from jax.sharding import Mesh
from jax.sharding import PartitionSpec as P

HARM = 8
PTS = ("pts_0", "pts_1", "pts_2")
PTS_TM = ("pts_0", "pts_1", "pts_2", "tm")


year_days = 365.25


def sent_to_all(shard, axis):
    count = lax.axis_size(axis)
    return lax.all_to_all(
        jnp.broadcast_to(shard[None], (count, *shard.shape)), axis, 0, 0, tiled=True
    )


def of_everyone(shard, axis):
    return sent_to_all(shard, axis).sum(axis=0)


def in_blocks(shard, dim, count):
    before, after = (shard.shape[:dim], shard.shape[dim + 1 :])
    return jnp.moveaxis(shard.reshape(*before, count, -1, *after), dim, 0)


def summed_on_arrival(shard, axis, dim):
    parts = in_blocks(shard, dim, lax.axis_size(axis))
    arrived = lax.all_to_all(parts, axis, split_axis=0, concat_axis=0, tiled=True)
    return arrived.sum(axis=0)


def padded_to(lines, count):
    spare = -len(lines) % count
    return jnp.pad(lines, [(0, spare)] + [(0, 0)] * (lines.ndim - 1))


def in_order(parts, dim):
    parts = jnp.moveaxis(parts, 0, dim)
    dims = parts.shape
    return parts.reshape(*dims[:dim], dims[dim] * dims[dim + 1], *dims[dim + 2 :])


def gathered_by_axis(shard, axes, dim):
    far, near = axes
    parts = sent_to_all(sent_to_all(shard, far), near)
    return in_order(parts.swapaxes(0, 1).reshape(-1, *shard.shape), dim)


def sum_by_axis(shard, axes, dim):
    far, near = axes
    own = summed_on_arrival(in_blocks(shard, dim, lax.axis_size(far)), near, dim + 1)
    return jnp.sum(lax.all_to_all(own, far, 0, 0, tiled=True), axis=0)


def sum_by_parts(shard, axes):
    lines = shard.reshape(-1)
    padded = padded_to(lines, lax.axis_size(axes[0]) * lax.axis_size(axes[1]))
    whole = gathered_by_axis(sum_by_axis(padded, axes, 0), axes, 0)
    return lax.slice_in_dim(whole, 0, len(lines)).reshape(shard.shape)


def harmonic_table(day_number):
    phase_base = day_number.astype(jnp.float32)
    columns = [jnp.ones_like(phase_base)]
    for order in range(1, HARM + 1):
        phase = 2.0 * math.pi * order / year_days * phase_base
        columns.append(jnp.cos(phase))
        columns.append(jnp.sin(phase))
    return jnp.stack(columns, 0)


def normal_solve(factor_low, values):
    forward = lax.linalg.triangular_solve(factor_low, values, left_side=True, lower=True)
    return lax.linalg.triangular_solve(
        factor_low, forward, left_side=True, lower=True, transpose_a=True
    )


def on_device(precip, thresholds, bin_index, test_matrix):
    highest = lax.Precision.HIGHEST
    tm_count = lax.axis_size("tm")
    tm_place = lax.axis_index("tm")
    days_local, points_local = precip.shape
    days_total = days_local * tm_count
    points_total = points_local * lax.axis_size(PTS)
    full_table = harmonic_table(jnp.arange(days_total, dtype=jnp.int32))
    normal = jnp.dot(full_table, full_table.T, precision=highest)
    normal_low = jnp.linalg.cholesky(normal)
    one_hot = (
        bin_index[:, None] == jnp.arange(thresholds.shape[0], dtype=jnp.int32)[None, :]
    ).astype(jnp.float32)
    level_local = jnp.dot(one_hot, thresholds, precision=highest)
    local_table = harmonic_table(tm_place * days_local + jnp.arange(days_local, dtype=jnp.int32))
    partial_proj = jnp.dot(local_table, precip, precision=highest)
    projections = of_everyone(partial_proj, "tm")
    coefficients = normal_solve(normal_low, projections)
    anomaly = precip - lax.dot_general(
        local_table, coefficients, (((0,), (0,)), ((), ())), precision=highest
    )
    excess = jnp.maximum(anomaly - level_local[None, :], 0.0)
    sketch = summed_on_arrival(
        lax.dot_general(excess, test_matrix, (((0,), (0,)), ((), ())), precision=highest), "tm", 0
    )
    local_cross = jnp.dot(sketch.T, sketch, precision=highest)
    cross = sum_by_parts(local_cross, ("tm", ("pts_0", "pts_1", "pts_2"))) / points_total
    lower = jnp.linalg.cholesky(cross)
    basis = lax.linalg.triangular_solve(
        lower, sketch, left_side=False, lower=True, transpose_a=True
    )
    return (basis, lower.T)


def solution(mesh):
    split = Mesh(mesh.devices.reshape(mesh.shape["tm"], 4, 8, 2), ("tm", "pts_0", "pts_1", "pts_2"))
    return jax.shard_map(
        on_device,
        mesh=split,
        in_specs=(P("tm", PTS), P(), P(PTS), P("tm", None)),
        out_specs=(P(PTS_TM, None), P()),
        check_vma=False,
    )
```

profile of v0, /device:TPU:1, one launch (start us, length us, event | category | flops | bytes accessed | tf_op | source)
XLA Modules:
  0.0 198.6 jit_solution(5644238819500224285)
XLA Ops:
  0.7 0.1 fusion.38
  0.8 0.1 fusion.40
  0.8 0.1 fusion.42
  0.9 0.1 fusion.44
  0.9 0.1 fusion.46
  1.0 0.1 fusion.48
  1.1 0.1 fusion.50
  1.1 0.1 stack.4
  1.2 1.8 fusion.55
  3.0 1.0 broadcast_in_dim.11
  4.0 7.7 %all-to-all-start = ((f32[8,17,1024]{2,1,0:T(8,128)}), f32[8,17,1024]{2,1,0:T(8,128)S(1)}, u32[]{:S(2)}, u32[]{:S(2)}) async-start(f32[8,17,1024]{2,1,0:T(8,128)} %broadcast_in_dim.11), calls=%async_computation | async-start | bytes 1572864 | tf_op jit(solution)/shard_map/all_to_all | solution.py:19
  11.7 0.2 fusion.20
  11.9 0.2 fusion.22
  12.2 0.2 fusion.24
  12.4 0.2 fusion.26
  12.7 0.2 fusion.28
  12.9 0.2 fusion.30
  13.2 0.2 fusion.32
  13.4 0.2 fusion.34
  13.7 0.2 stack.5
  14.0 0.3 fusion.54
  14.2 0.1 copy.26
  14.4 1.5 cholesky.60
  16.0 0.6 compare_reduce_fusion.2
  16.6 0.6 fusion.14
  17.3 1.3 custom-call.22
  18.6 0.4 fusion.2
  19.0 13.6 %all-to-all-done = f32[8,17,1024]{2,1,0:T(8,128)S(1)} async-done(((f32[8,17,1024]{2,1,0:T(8,128)}), f32[8,17,1024]{2,1,0:T(8,128)S(1)}, u32[]{:S(2)}, u32[]{:S(2)}) %all-to-all-start) | async-done | bytes 557088 | tf_op jit(solution)/shard_map/all_to_all | solution.py:19
  32.7 0.3 fusion.17
  33.0 0.2 fusion.15
  33.3 1.1 fusion.1
  34.4 1.8 fusion.56
  36.2 27.2 %all_to_all.35 = f32[8,128,256]{2,1,0:T(8,128)S(1)} all-to-all(f32[8,128,256]{2,1,0:T(8,128)S(1)} %bitcast.68), channel_id=1, replica_groups=mesh['tm'=8,'pts_0'=4,'pts_1'=8,'pts_2'=2] {'tm'}, dimensions={0} | all-to-all | bytes 2097152 | tf_op jit(solution)/shard_map/all_to_all | solution.py:35
  63.5 0.1 reduce_sum.37
  63.5 0.4 fusion.57
  64.0 0.2 copy.35
  64.1 32.5 %all_to_all.36 = f32[64,8,128]{2,1,0:T(8,128)S(1)} all-to-all(f32[64,8,128]{2,1,0:T(8,128)S(1)} %bitcast.69), channel_id=1, replica_groups=mesh['tm'=8,'pts_0'=4,'pts_1'=8,'pts_2'=2] {'pts_0','pts_1','pts_2'}, dimensions={0} | all-to-all | bytes 524288 | tf_op jit(solution)/shard_map/all_to_all | solution.py:35
  96.7 0.1 reduce_sum.38
  96.7 8.9 %all_to_all.37 = f32[8,1,128]{2,1,0:T(1,128)S(1)} all-to-all(f32[8,1,128]{2,1,0:T(1,128)S(1)} %bitcast.70), channel_id=1, replica_groups=mesh['tm'=8,'pts_0'=4,'pts_1'=8,'pts_2'=2] {'tm'}, dimensions={0} | all-to-all | bytes 8192 | tf_op jit(solution)/shard_map/all_to_all | solution.py:59
  105.7 8.9 %all_to_all.38 = f32[8,1,128]{2,1,0:T(1,128)S(1)} all-to-all(f32[8,1,128]{2,1,0:T(1,128)S(1)} %broadcast_in_dim.12), channel_id=1, replica_groups=mesh['tm'=8,'pts_0'=4,'pts_1'=8,'pts_2'=2] {'tm'}, dimensions={0} | all-to-all | bytes 8192 | tf_op jit(solution)/shard_map/all_to_all | solution.py:19
  114.6 0.7 broadcast_in_dim.14
  115.3 8.3 %all-to-all-start.5 = ((f32[64,8,128]{2,1,0:T(8,128)}), f32[64,8,128]{2,1,0:T(8,128)S(1)}, u32[]{:S(2)}, u32[]{:S(2)}) async-start(f32[64,8,128]{2,1,0:T(8,128)} %broadcast_in_dim.14), calls=%async_computation.5 | async-start | bytes 524288 | tf_op jit(solution)/shard_map/all_to_all | solution.py:19
  123.6 12.0 %all-to-all-done.5 = f32[64,8,128]{2,1,0:T(8,128)S(1)} async-done(((f32[64,8,128]{2,1,0:T(8,128)}), f32[64,8,128]{2,1,0:T(8,128)S(1)}, u32[]{:S(2)}, u32[]{:S(2)}) %all-to-all-start.5) | async-done | bytes 262176 | tf_op jit(solution)/shard_map/all_to_all | solution.py:19
  135.7 0.1 div.31
  135.8 0.1 copy.30
  136.0 11.7 %cholesky.123 = f32[128,128]{1,0:T(8,128)S(1)} custom-call(f32[128,128]{1,0:T(8,128)S(1)} %cholesky.153), custom_call_target="Cholesky" | custom-call | tf_op jit(solution)/shard_map/jit(cholesky)/cholesky | solution.py:113
  147.7 9.8 %custom-call.23 = f32[1,128,128]{1,2,0:T(8,128)S(1)} custom-call(f32[1,128,128]{2,1,0:T(8,128)S(1)} %get-tuple-element.35), custom_call_target="InvertDiagBlocksLowerTriangular" | custom-call | tf_op jit(solution)/shard_map/jit(cholesky)/cholesky | solution.py:113
  157.6 0.2 constant_dynamic-update-slice_fusion.1
  157.8 0.3 convolution_subtract_fusion.2
  158.0 11.7 %cholesky.140 = f32[128,128]{1,0:T(8,128)S(1)} custom-call(f32[128,128]{1,0:T(8,128)S(1)} %convolution_subtract_fusion.2), custom_call_target="Cholesky" | custom-call | tf_op jit(solution)/shard_map/jit(cholesky)/cholesky | solution.py:113
  169.8 0.6 compare_reduce_fusion
  170.4 0.6 compare_reduce_fusion.1
  172.3 0.1 triangular_solve.97
  172.4 3.8 %while.1 = (s32[]{:T(128)}, f32[256,256]{1,0:T(8,128)S(1)}, s32[2,2]{1,0:T(2,128)S(1)}, f32[2,128,128]{2,1,0:T(8,128)S(1)}, s32[]{:T(128)}) while((s32[]{:T(128)}, f32[256,256]{1,0:T(8,128)S(1)}, s32[2,2]{1,0:T(2,128)S(1)}, f32[2,128,128]{2,1,0:T(8,128)S(1)}, s32[]{:T(128)}) %tuple.48), condition=%wide.while_cond, body=%wide.while_body.sunk | while | flops 2 | bytes 131181 | solution.py:114
  172.4 0.6 fusion.75
  173.0 1.3 bitcast_dynamic-update-slice_fusion.2
  174.3 0.6 fusion.75
  174.9 1.3 bitcast_dynamic-update-slice_fusion.2
  176.2 19.9 %custom-call.24 = f32[2,128,128]{1,2,0:T(8,128)S(1)} custom-call(f32[2,128,128]{2,1,0:T(8,128)S(1)} %get-tuple-element.9), custom_call_target="InvertDiagBlocksLowerTriangular" | custom-call | tf_op jit(solution)/shard_map/triangular_solve | solution.py:114
  196.1 0.3 fusion.9
  196.4 0.3 convolution_subtract_fusion.1
  196.7 0.3 fusion.7
  197.0 0.8 copy.31
  197.8 0.8 copy.32
  (30 shorter events, 0.5 us)
Async XLA Ops:
  0.6 33.7 %copy-start = (f32[256,256]{1,0:T(8,128)S(1)}, f32[256,256]{1,0:T(8,128)}, u32[]{:S(2)}) copy-start(f32[256,256]{1,0:T(8,128)} %param.7) | copy-start | bytes 786436
  4.0 28.7 %all-to-all-start = ((f32[8,17,1024]{2,1,0:T(8,128)}), f32[8,17,1024]{2,1,0:T(8,128)S(1)}, u32[]{:S(2)}, u32[]{:S(2)}) async-start(f32[8,17,1024]{2,1,0:T(8,128)} %broadcast_in_dim.11), calls=%async_computation | async-start | bytes 1572864 | tf_op jit(solution)/shard_map/all_to_all | solution.py:19
  13.7 4.9 %copy-start.2 = (s32[1024]{0:T(1024)S(1)}, s32[1024]{0:T(1024)}, u32[]{:S(2)}) copy-start(s32[1024]{0:T(1024)} %param.6) | copy-start | bytes 12292
  13.7 4.9 %copy-start.3 = (f32[64]{0:T(128)S(1)}, f32[64]{0:T(128)}, u32[]{:S(2)}) copy-start(f32[64]{0:T(128)} %param.5) | copy-start | bytes 772
  13.9 19.3 %copy-start.1 = (f32[256,1024]{1,0:T(8,128)S(1)}, f32[256,1024]{1,0:T(8,128)}, u32[]{:S(2)}) copy-start(f32[256,1024]{1,0:T(8,128)} %param.4) | copy-start | bytes 3145732
  115.3 20.3 %all-to-all-start.5 = ((f32[64,8,128]{2,1,0:T(8,128)}), f32[64,8,128]{2,1,0:T(8,128)S(1)}, u32[]{:S(2)}, u32[]{:S(2)}) async-start(f32[64,8,128]{2,1,0:T(8,128)} %broadcast_in_dim.14), calls=%async_computation.5 | async-start | bytes 524288 | tf_op jit(solution)/shard_map/all_to_all | solution.py:19
where the time goes:
time: 199 us
  blocking collectives  77.6 us (39%)
  other arithmetic  61.4 us (31%)
  waiting for transfers between devices  25.6 us (13%)
  starting transfers between devices  16 us (8%)
  local copies, waits for them, and re-layouts  8.09 us (4%)
  matrix products  7.73 us (4%)
  between operations  2.22 us (1%)
    all_to_all x2, blocking collectives, summed_on_arrival(): lax.all_to_all(parts, axis, split_axis=0, concat_axis=0, tiled=True)  59.8 us
    another operation x7, other arithmetic, on_device(): lower = jnp.linalg.cholesky(cross)  34.6 us
    all_to_all x2, waiting for transfers between devices, sent_to_all(): lax.all_to_all(jnp.broadcast_to(shard[None], (count, *shard.shape)), axis...  25.6 us
    another operation x3, other arithmetic, on_device(): lax.linalg.triangular_solve(lower, sketch, left_side=False, lower=True, t...  19.9 us
    all_to_all x2, starting transfers between devices, sent_to_all(): lax.all_to_all(jnp.broadcast_to(shard[None], (count, *shard.shape)), axis...  16 us
    all_to_all x1, blocking collectives, sum_by_axis(): return jnp.sum(lax.all_to_all(own, far, 0, 0, tiled=True), axis=0)  8.89 us
    all_to_all x1, blocking collectives, sent_to_all(): lax.all_to_all(jnp.broadcast_to(shard[None], (count, *shard.shape)), axis...  8.89 us
  transfers between devices with their start and end apart: 2, of which 2 were waited for; matrix products, arithmetic and copies ran while one was open for 4% of the time, Pallas kernels for 0%

commit v1 on v0

v1 whole, which is shorter than its diff:
```python
import functools
import math

import jax
import jax.numpy as jnp
import numpy as np
from jax import lax
from jax.experimental import pallas as pl
from jax.experimental.pallas import tpu as pltpu
from jax.sharding import Mesh
from jax.sharding import PartitionSpec as P

HARM = 8
YEAR_DAYS = 365.25
ROWS = 24
PTS = ("pts_0", "pts_1", "pts_2")
PTS_TM = ("pts_0", "pts_1", "pts_2", "tm")
MESH = pl.DeviceIdType.MESH
HIGHEST = lax.Precision.HIGHEST


def harmonic_basis(days):
    day = np.arange(days, dtype=np.float32)
    columns = [np.ones(days)]
    for order in range(1, HARM + 1):
        phase = (np.float32(2.0 * math.pi * order / YEAR_DAYS) * day).astype(np.float64)
        columns += [np.cos(phase), np.sin(phase)]
    table = np.stack(columns)
    return np.linalg.solve(np.linalg.cholesky(table @ table.T), table)


def dot(a, b, dims):
    return lax.dot_general(
        a, b, (dims, ((), ())), precision=HIGHEST, preferred_element_type=jnp.float32
    )


def gather_kernel(
    scale,
    precip,
    table,
    test,
    bins,
    thresholds,
    sketch_out,
    cross_out,
    *scratch,
):
    (
        test_t,
        proj_out,
        proj_in,
        coef,
        level,
        sketch,
        ring,
        cross,
        core_in,
        y_in,
        z_in,
        x_in,
        total,
        proj_sem,
        coef_sem,
        ring_sem,
        core_sem,
        y_sem,
        z_sem,
        x_sem,
        gather_sem,
        join_sem,
    ) = scratch
    y = lax.axis_index("tm")
    x = lax.axis_index("pts_0")
    z = lax.axis_index("pts_1")
    c = lax.axis_index("pts_2")
    n_y, n_x, n_z = (lax.axis_size(a) for a in ("tm", "pts_0", "pts_1"))
    sends = []

    def send(src, dst, sem, device):
        copy = pltpu.make_async_remote_copy(
            src_ref=src,
            dst_ref=dst,
            send_sem=sem.at[0],
            recv_sem=sem.at[1],
            device_id=device,
            device_id_type=MESH,
        )
        copy.start()
        sends.append(copy)
        return copy

    y_at = lambda o: lax.rem(y + o + n_y, n_y)
    x_at = lambda o: lax.rem(x + o + n_x, n_x)
    z_at = lambda o: lax.rem(z + o + n_z, n_z)

    barrier = pltpu.get_barrier_semaphore()
    others = [{"tm": y_at(o)} for o in range(1, n_y)]
    others += [{"pts_0": x_at(o)} for o in range(1, n_x)]
    others += [{"pts_1": z_at(o)} for o in range(1, n_z)]
    others += [{"pts_2": 1 - c}]
    for other in others:
        pl.semaphore_signal(barrier, inc=1, device_id=other, device_id_type=MESH)

    mine = table[y]
    proj = dot(mine, precip[...], ((1,), (0,)))
    for r in range(n_y):
        proj_out[r] = proj[:, 128 * r : 128 * (r + 1)]
    pl.semaphore_wait(barrier, len(others))
    arrivals = []
    for o in [4, 3, 5, 2, 6, 1, 7]:
        arrivals.append(send(proj_out.at[y_at(o)], proj_in.at[o], proj_sem.at[o], {"tm": y_at(o)}))
    test_t[...] = test[...].T
    found = bins[...]
    value = jnp.zeros(found.shape, jnp.float32)
    for k in range(thresholds.shape[0]):
        value = jnp.where(found == k, thresholds[k], value)
    level[...] = value
    for copy in arrivals:
        copy.wait_recv()
    own = proj_out[y]
    for o in range(1, n_y):
        own = own + proj_in[o]
    coef[y] = own
    arrivals = []
    for o in [4, 3, 5, 2, 6, 1, 7]:
        arrivals.append(send(coef.at[y], coef.at[y], coef_sem.at[o], {"tm": y_at(o)}))
    for copy in arrivals:
        copy.wait_recv()

    def partial(o):
        r = y_at(o)
        fit = dot(mine, coef[r], ((0,), (0,)))
        data = precip[:, pl.ds(pl.multiple_of(128 * r, 128), 128)]
        excess = jnp.maximum(data - fit - level[pl.ds(r, 1), :], 0.0)
        sketch[o % n_y] = dot(test_t[...], excess, ((1,), (0,)))

    n_p = ring.shape[1] // 2
    piece = 128 // n_p

    def chain(way, q, step):
        hops = 4 if (q < n_p) == (way == 0) else 3
        if step > hops:
            return None
        o = hops + 1 - step
        return o if way == 0 else -o

    def rows_of(q):
        return pl.ds(q * piece, piece)

    def hop(way, q, step):
        o = chain(way, q, step) % n_y
        src = sketch.at[o, rows_of(q)] if step == 1 else ring.at[way, q, step - 2]
        return send(
            src,
            ring.at[way, q, step - 1],
            ring_sem.at[way, q, step - 1],
            {"tm": y_at(1 if way == 0 else -1)},
        )

    order = [(w, q) for q in range(n_p) for w in (0, 1)]
    long = [(w, q if w == 0 else q + n_p) for w, q in order]
    short = [(w, q + n_p if w == 0 else q) for w, q in order]
    moving = {}
    partial(4)
    for w, q in long:
        moving[w, q] = hop(w, q, 1)
    partial(3)
    for w, q in short:
        if w == 0:
            moving[w, q] = hop(w, q, 1)
    partial(-3)
    for w, q in short:
        if w == 1:
            moving[w, q] = hop(w, q, 1)
    partial(2)
    partial(-2)
    for step in (2, 3, 4):
        for w, q in long + short:
            o = chain(w, q, step)
            if o is None:
                continue
            moving[w, q].wait_recv()
            ring[w, q, step - 2] += sketch[o % n_y, rows_of(q)]
            moving[w, q] = hop(w, q, step)
        if step == 2:
            partial(1)
            partial(-1)
            partial(0)
    for q in range(2 * n_p):
        value = sketch[0, rows_of(q)]
        for w in (0, 1):
            hops = 4 if (w, q) in long else 3
            moving[w, q].wait_recv()
            value = value + ring[w, q, hops - 1]
        sketch_out[rows_of(q)] = value

    upper = sketch_out[:128]
    lower = sketch_out[128:]
    cross[:128] = dot(upper, upper, ((1,), (1,))) * scale
    cross[128:256] = dot(lower, upper, ((1,), (1,))) * scale
    cross[256:] = dot(lower, lower, ((1,), (1,))) * scale
    half = cross.shape[0] // 2
    part = half // n_y
    copy = send(
        cross.at[pl.ds(pl.multiple_of((1 - c) * half, 8), half)], core_in, core_sem, {"pts_2": 1 - c}
    )
    copy.wait_recv()
    core_in[...] += cross[pl.ds(pl.multiple_of(c * half, 8), half)]
    arrivals = []
    for o in [4, 3, 5, 2, 6, 1, 7]:
        arrivals.append(
            send(
                core_in.at[pl.ds(pl.multiple_of(y_at(o) * part, 8), part)],
                y_in.at[o],
                y_sem.at[o],
                {"tm": y_at(o)},
            )
        )
    for copy in arrivals:
        copy.wait_recv()
    own = core_in[pl.ds(pl.multiple_of(y * part, 8), part)]
    for o in range(1, n_y):
        own = own + y_in[o]
    z_in[z] = own
    arrivals = []
    for o in [4, 3, 5, 2, 6, 1, 7]:
        arrivals.append(send(z_in.at[z], z_in.at[z], z_sem.at[o], {"pts_1": z_at(o)}))
    for copy in arrivals:
        copy.wait_recv()
    own = z_in[0]
    for o in range(1, n_z):
        own = own + z_in[o]
    x_in[x] = own
    arrivals = []
    for o in [2, 1, 3]:
        arrivals.append(send(x_in.at[x], x_in.at[x], x_sem.at[o], {"pts_0": x_at(o)}))
    for copy in arrivals:
        copy.wait_recv()
    own = x_in[0]
    for o in range(1, n_x):
        own = own + x_in[o]
    place = pl.ds(pl.multiple_of(c * half + y * part, 8), part)
    total[place] = own
    arrivals = []
    for o in [4, 3, 5, 2, 6, 1, 7]:
        arrivals.append(send(total.at[place], total.at[place], gather_sem.at[o], {"tm": y_at(o)}))
    for copy in arrivals:
        copy.wait_recv()
    place = pl.ds(pl.multiple_of(c * half, 8), half)
    send(total.at[place], total.at[place], join_sem, {"pts_2": 1 - c}).wait_recv()
    cross_out[...] = total[...]
    for copy in sends:
        copy.wait_send()


PIECES = 2


def gathered(precip, table, test, bins, thresholds, points_total):
    vmem = pl.BlockSpec(memory_space=pltpu.VMEM)
    smem = pl.BlockSpec(memory_space=pltpu.SMEM)
    f32 = jnp.float32
    dma = pltpu.SemaphoreType.DMA
    half = 192
    part = 24
    return pl.pallas_call(
        functools.partial(gather_kernel, 1.0 / points_total),
        out_shape=(
            jax.ShapeDtypeStruct((256, 128), f32),
            jax.ShapeDtypeStruct((384, 128), f32),
        ),
        in_specs=[vmem, vmem, vmem, vmem, smem],
        out_specs=(vmem, vmem),
        scratch_shapes=[
            pltpu.VMEM((256, 256), f32),
            pltpu.VMEM((8, ROWS, 128), f32),
            pltpu.VMEM((8, ROWS, 128), f32),
            pltpu.VMEM((8, ROWS, 128), f32),
            pltpu.VMEM((8, 128), f32),
            pltpu.VMEM((8, 256, 128), f32),
            pltpu.VMEM((2, 2 * PIECES, 4, 128 // PIECES, 128), f32),
            pltpu.VMEM((384, 128), f32),
            pltpu.VMEM((half, 128), f32),
            pltpu.VMEM((8, part, 128), f32),
            pltpu.VMEM((8, part, 128), f32),
            pltpu.VMEM((4, part, 128), f32),
            pltpu.VMEM((384, 128), f32),
            dma((8, 2)),
            dma((8, 2)),
            dma((2, 2 * PIECES, 4, 2)),
            dma((2,)),
            dma((8, 2)),
            dma((8, 2)),
            dma((4, 2)),
            dma((8, 2)),
            dma((2,)),
        ],
        compiler_params=pltpu.CompilerParams(
            collective_id=0, has_side_effects=True, vmem_limit_bytes=40 << 20
        ),
        name="gathered",
    )(precip, table, test, bins, thresholds)


def on_device(precip, thresholds, bin_index, test_matrix):
    days = precip.shape[0] * lax.axis_size("tm")
    points_total = precip.shape[1] * lax.axis_size(PTS)
    rows = harmonic_basis(days)
    table = np.zeros((lax.axis_size("tm"), ROWS, precip.shape[0]), np.float32)
    table[:, : len(rows)] = rows.reshape(len(rows), -1, precip.shape[0]).swapaxes(0, 1)
    sketch_t, blocks = gathered(
        precip, table, test_matrix, bin_index.reshape(-1, 128), thresholds, points_total
    )
    cross = jnp.concatenate(
        [
            jnp.concatenate([blocks[:128], blocks[128:256].T], 1),
            jnp.concatenate([blocks[128:256], blocks[256:]], 1),
        ],
        0,
    )
    lower = jnp.linalg.cholesky(cross)
    basis = lax.linalg.triangular_solve(
        lower, sketch_t, left_side=True, lower=True
    ).T
    return (basis, lower.T)


def solution(mesh):
    split = Mesh(mesh.devices.reshape(mesh.shape["tm"], 4, 8, 2), ("tm", *PTS))
    return jax.shard_map(
        on_device,
        mesh=split,
        in_specs=(P("tm", PTS), P(), P(PTS), P("tm", None)),
        out_specs=(P(PTS_TM, None), P()),
        check_vma=False,
    )
```

time: 199 us -> 131 us (0.66)
  blocking collectives: 77.6 us -> 0 us
  Pallas kernels: 0 us -> 63 us
  waiting for transfers between devices: 25.6 us -> 0 us
  starting transfers between devices: 16 us -> 0 us
  other arithmetic: 61.4 us -> 53.8 us
  matrix products: 7.73 us -> 1.24 us
  local copies, waits for them, and re-layouts: 8.09 us -> 10.4 us
    all_to_all x4 -> x0, blocking collectives: 77.6 us -> none  [the longest x2 59.8 us: summed_on_arrival(): lax.all_to_all(parts, axis, split_axis=0, concat_axis=0, tiled=True)]
    pallas_call x0 -> x1, Pallas kernels: none -> 63 us  [gathered(): pl.pallas_call(functools.partial(gather_kernel, 1.0 / points_total), out_...]
    all_to_all x2 -> x0, waiting for transfers between devices: 25.6 us -> none  [sent_to_all(): lax.all_to_all(jnp.broadcast_to(shard[None], (count, *shard.shape)), axis...]
    all_to_all x2 -> x0, starting transfers between devices: 16 us -> none  [sent_to_all(): lax.all_to_all(jnp.broadcast_to(shard[None], (count, *shard.shape)), axis...]
    dot_general x6 -> x0, matrix products: 5.89 us -> none  [the longest x1 1.84 us: on_device(): partial_proj = jnp.dot(local_table, precip, precision=highest)]
    another operation x8 -> x2, other arithmetic: 24.1 us -> 19.7 us  [on_device(): lax.linalg.triangular_solve(lower, sketch_t, left_side=True, lower=True)]
    unnamed x10 -> x12, local copies, waits for them, and re-layouts: 1.62 us -> 6.03 us
    sin x16 -> x0, other arithmetic: 2.41 us -> none  [harmonic_table(): columns.append(jnp.sin(phase))]
  transfers between devices with their start and end apart: 2 -> 0, of which waited for: 2 -> 0; matrix products, arithmetic and copies ran while one was open for 4% -> 0% of each run, Pallas kernels for 0% -> 0%
where the time goes in v1:
time: 131 us
  Pallas kernels  63 us (48%)
  other arithmetic  53.8 us (41%)
  local copies, waits for them, and re-layouts  10.4 us (8%)
  between operations  2.11 us (2%)
    pallas_call x1, Pallas kernels, gathered(): pl.pallas_call(functools.partial(gather_kernel, 1.0 / points_total), out_...  63 us
    another operation x6, other arithmetic, on_device(): lower = jnp.linalg.cholesky(cross)  34.1 us
    another operation x2, other arithmetic, on_device(): lax.linalg.triangular_solve(lower, sketch_t, left_side=True, lower=True)  19.7 us
    unnamed x12, local copies, waits for them, and re-layouts  6.03 us
    another operation x6, local copies, waits for them, and re-layouts  3.93 us

profile of v1, /device:TPU:1, one launch (start us, length us, event | category | flops | bytes accessed | tf_op | source)
XLA Modules:
  0.0 130.6 jit_solution(15533845992308329794)
XLA Ops:
  0.6 0.0 copy-start.4
  0.6 0.6 copy-done.4
  1.3 0.0 copy-start
  1.3 1.2 copy-done
  2.5 0.0 copy-start.1
  2.5 0.9 copy-done.1
  3.5 0.0 copy-start.2
  3.5 0.9 copy-done.2
  4.4 0.0 copy-start.3
  4.4 0.7 copy-done.3
  5.1 63.0 %gathered.1 = (f32[256,128]{1,0:T(8,128)S(1)}, f32[384,128]{1,0:T(8,128)S(1)}) custom-call(f32[256,1024]{1,0:T(8,128)S(1)} %copy-done, f32[8,24,256]{2,1,0:T(8,128)S(1)} %copy-done.2, f32[256,256]{1,0:T(8,128)S(1)} %copy-done.1, s32[8,128]{1,0:T(8,128)S(1)} %bitcast.38, f32[64]{0:T(128)S(1)} %copy-done.4), custom_call_target="tpu_custom_call" | custom-call | tf_op jit(solution)/shard_map/gathered/pallas_call | solution.py:267
  68.1 0.1 copy.7
  68.2 0.1 copy.9
  68.4 0.1 copy.10
  68.6 11.7 %cholesky.50 = f32[128,128]{1,0:T(8,128)S(1)} custom-call(f32[128,128]{1,0:T(8,128)S(1)} %cholesky.118), custom_call_target="Cholesky" | custom-call | tf_op jit(solution)/shard_map/jit(cholesky)/cholesky | solution.py:322
  80.3 9.8 %custom-call.14 = f32[1,128,128]{1,2,0:T(8,128)S(1)} custom-call(f32[1,128,128]{2,1,0:T(8,128)S(1)} %get-tuple-element.34), custom_call_target="InvertDiagBlocksLowerTriangular" | custom-call | tf_op jit(solution)/shard_map/jit(cholesky)/cholesky | solution.py:322
  90.2 0.2 constant_dynamic-update-slice_fusion.1
  90.4 0.3 convolution_subtract_fusion.1
  90.6 11.8 %cholesky.105 = f32[128,128]{1,0:T(8,128)S(1)} custom-call(f32[128,128]{1,0:T(8,128)S(1)} %convolution_subtract_fusion.1), custom_call_target="Cholesky" | custom-call | tf_op jit(solution)/shard_map/jit(cholesky)/cholesky | solution.py:322
  102.5 0.6 compare_reduce_fusion
  104.5 0.1 triangular_solve.57
  104.6 4.0 %while.1 = (s32[]{:T(128)}, f32[256,256]{1,0:T(8,128)S(1)}, s32[2,2]{1,0:T(2,128)S(1)}, f32[2,128,128]{2,1,0:T(8,128)S(1)}, s32[]{:T(128)}) while((s32[]{:T(128)}, f32[256,256]{1,0:T(8,128)S(1)}, s32[2,2]{1,0:T(2,128)S(1)}, f32[2,128,128]{2,1,0:T(8,128)S(1)}, s32[]{:T(128)}) %tuple.31), condition=%wide.while_cond, body=%wide.while_body.sunk | while | flops 2 | bytes 131181 | solution.py:323
  104.6 0.6 fusion.16
  105.2 1.4 %bitcast_dynamic-update-slice_fusion.2 = f32[2,128,128]{2,1,0:T(8,128)S(1)} fusion(f32[2,128,128]{2,1,0:T(8,128)S(1)} %get-tuple-element.76, s32[]{:T(128)} %get-tuple-element.73, f32[256,256]{1,0:T(8,128)S(1)} %get-tuple-element.79, s32[]{:T(128)} %bitcast.36, s32[]{:T(128)} %bitcast.37), kind=kLoop, calls=%fused_computation.clone.1 | loop fusion | bytes 131084 | tf_op jit(solution)/shard_map/triangular_solve
  106.6 0.6 fusion.16
  107.1 1.4 %bitcast_dynamic-update-slice_fusion.2 = f32[2,128,128]{2,1,0:T(8,128)S(1)} fusion(f32[2,128,128]{2,1,0:T(8,128)S(1)} %get-tuple-element.76, s32[]{:T(128)} %get-tuple-element.73, f32[256,256]{1,0:T(8,128)S(1)} %get-tuple-element.79, s32[]{:T(128)} %bitcast.36, s32[]{:T(128)} %bitcast.37), kind=kLoop, calls=%fused_computation.clone.1 | loop fusion | bytes 131084 | tf_op jit(solution)/shard_map/triangular_solve
  108.5 19.7 %custom-call.15 = f32[2,128,128]{1,2,0:T(8,128)S(1)} custom-call(f32[2,128,128]{2,1,0:T(8,128)S(1)} %get-tuple-element.13), custom_call_target="InvertDiagBlocksLowerTriangular" | custom-call | tf_op jit(solution)/shard_map/triangular_solve | solution.py:323
  128.2 0.3 fusion.5
  128.5 0.2 convolution_subtract_fusion
  128.7 0.3 fusion.4
  129.0 0.8 copy.11
  129.8 0.8 copy.12
  (15 shorter events, 0.2 us)
Async XLA Ops:
  0.6 0.7 copy-start.4
  1.3 1.2 copy-start
  2.5 0.9 copy-start.1
  3.5 0.9 copy-start.2
  4.4 0.7 copy-start.3

commit v2 on v1

--- a/solution.py
+++ b/solution.py
@@ -198,7 +198,7 @@
     upper = sketch_out[:128]
     lower = sketch_out[128:]
     cross[:128] = dot(upper, upper, ((1,), (1,))) * scale
-    cross[128:256] = dot(lower, upper, ((1,), (1,))) * scale
+    cross[128:256] = dot(upper, lower, ((1,), (1,))) * scale
     cross[256:] = dot(lower, lower, ((1,), (1,))) * scale
     half = cross.shape[0] // 2
     part = half // n_y
@@ -303,6 +303,106 @@
     )(precip, table, test, bins, thresholds)
 
 
+def terms(a):
+    first = a.astype(jnp.bfloat16)
+    rest = a - first.astype(jnp.float32)
+    second = rest.astype(jnp.bfloat16)
+    return first, second, (rest - second.astype(jnp.float32)).astype(jnp.bfloat16)
+
+
+BLOCK = 32
+
+
+def factor_kernel(cross, sketch, basis_out, factor_out, work):
+    work[:128, :128] = cross[:128]
+    work[:128, 128:256] = cross[128:256]
+    work[128:, 128:256] = cross[256:]
+    work[:, 256:] = sketch[...]
+    factor_out[128:, :128] = jnp.zeros((128, 128), jnp.float32)
+    sub = lax.broadcasted_iota(jnp.int32, (8, 128), 0)
+    lane = lax.broadcasted_iota(jnp.int32, (8, 128), 1)
+    wide = lambda row: jnp.broadcast_to(row, (8, 128))
+    groups = BLOCK // 8
+    for first in range(0, 256, BLOCK):
+        tile, start = first // 128, first % 128
+        tiles = range(tile, 3)
+        rows = {
+            (g, u): work[first + 8 * g : first + 8 * g + 8, 128 * u : 128 * u + 128]
+            for g in range(groups)
+            for u in tiles
+        }
+        done = {}
+        for g in range(groups):
+            at = start + 8 * g
+            column = {
+                (j, h): wide(rows[h, tile][:, at + j : at + j + 1])
+                for j in range(8)
+                for h in range(g, groups)
+            }
+            root = jnp.zeros((8, 128), jnp.float32)
+            for j in range(8):
+                pivot = wide(column[j, g][j : j + 1])
+                inverse = 1.0 / pivot
+                root = jnp.where(sub == j, lax.rsqrt(pivot), root)
+                ratio = {h: column[j, h] * inverse for h in range(g, groups)}
+                for k in range(j + 1, 8):
+                    value = wide(column[j, g][k : k + 1])
+                    for h in range(g, groups):
+                        column[k, h] = column[k, h] - ratio[h] * value
+                ratio[g] = jnp.where(sub > j, ratio[g], 0.0)
+                for u in tiles:
+                    row = wide(rows[g, u][j : j + 1])
+                    for h in range(g if j < 7 else g + 1, groups):
+                        rows[h, u] = rows[h, u] - ratio[h] * row
+            place = slice(first + 8 * g, first + 8 * g + 8)
+            for u in tiles:
+                value = rows[g, u] * root
+                if u == tile:
+                    value = jnp.where(lane >= at + sub, value, 0.0)
+                done[g, u] = value
+                if u < 2:
+                    factor_out[place, 128 * u : 128 * u + 128] = value
+                else:
+                    work[place, 256:] = value
+        after = first + BLOCK
+        if after >= 256:
+            break
+        base = 128 * tile
+        panel = jnp.concatenate(
+            [jnp.concatenate([done[g, u] for u in tiles], 1) for g in range(groups)], 0
+        )
+        one, two, three = terms(panel)
+        left = jnp.concatenate([one, one, two, two, one, three], 0)[:, : 256 - base].T
+        right = jnp.concatenate([one, two, one, two, three, one], 0)
+        ends = sorted({after, after + BLOCK, max(after, 128), 256})
+        for low, high in zip(ends, ends[1:]):
+            edge = 128 * (low // 128)
+            work[low:high, edge:] -= jnp.dot(
+                left[low - base : high - base],
+                right[:, edge - base :],
+                preferred_element_type=jnp.float32,
+            )
+    basis_out[:, :128] = work[:128, 256:].T
+    basis_out[:, 128:] = work[128:, 256:].T
+
+
+def factored(cross, sketch):
+    vmem = pl.BlockSpec(memory_space=pltpu.VMEM)
+    f32 = jnp.float32
+    return pl.pallas_call(
+        factor_kernel,
+        out_shape=(
+            jax.ShapeDtypeStruct((128, 256), f32),
+            jax.ShapeDtypeStruct((256, 256), f32),
+        ),
+        in_specs=[vmem, vmem],
+        out_specs=(vmem, vmem),
+        scratch_shapes=[pltpu.VMEM((256, 384), f32)],
+        compiler_params=pltpu.CompilerParams(vmem_limit_bytes=40 << 20),
+        name="factored",
+    )(cross, sketch)
+
+
 def on_device(precip, thresholds, bin_index, test_matrix):
     days = precip.shape[0] * lax.axis_size("tm")
     points_total = precip.shape[1] * lax.axis_size(PTS)
@@ -312,18 +412,7 @@
     sketch_t, blocks = gathered(
         precip, table, test_matrix, bin_index.reshape(-1, 128), thresholds, points_total
     )
-    cross = jnp.concatenate(
-        [
-            jnp.concatenate([blocks[:128], blocks[128:256].T], 1),
-            jnp.concatenate([blocks[128:256], blocks[256:]], 1),
-        ],
-        0,
-    )
-    lower = jnp.linalg.cholesky(cross)
-    basis = lax.linalg.triangular_solve(
-        lower, sketch_t, left_side=True, lower=True
-    ).T
-    return (basis, lower.T)
+    return factored(blocks, sketch_t)
 
 
 def solution(mesh):

time: 131 us -> 76.6 us (0.58)
  other arithmetic: 53.8 us -> 0 us
  Pallas kernels: 63 us -> 71.2 us
  local copies, waits for them, and re-layouts: 10.4 us -> 4.43 us
  between operations: 2.11 us -> 0.65 us
    another operation x8 -> x0, other arithmetic: 53.7 us -> none  [the longest x6 34.1 us: on_device(): lower = jnp.linalg.cholesky(cross)]
    pallas_call x0 -> x1, Pallas kernels: none -> 8.22 us  [factored(): pl.pallas_call(factor_kernel, out_shape=(jax.ShapeDtypeStruct((128, 256),...]
    another operation x9 -> x0, local copies, waits for them, and re-layouts: 4.02 us -> none
    unnamed x12 -> x10, local copies, waits for them, and re-layouts: 6.03 us -> 4.43 us
where the time goes in v2:
time: 76.6 us; the launch traced here: 76.3 us
  Pallas kernels  71.2 us (93%)
  local copies, waits for them, and re-layouts  4.43 us (6%)
    pallas_call x1, Pallas kernels, gathered(): pl.pallas_call(functools.partial(gather_kernel, 1.0 / points_total), out_...  63 us
    pallas_call x1, Pallas kernels, factored(): pl.pallas_call(factor_kernel, out_shape=(jax.ShapeDtypeStruct((128, 256),...  8.22 us
    unnamed x10, local copies, waits for them, and re-layouts  4.43 us

profile of v2, /device:TPU:1, one launch (start us, length us, event | category | flops | bytes accessed | tf_op | source)
XLA Modules:
  0.0 76.3 jit_solution(4859489014606809221)
XLA Ops:
  0.6 0.0 copy-start.4
  0.6 0.6 copy-done.4
  1.3 0.0 copy-start
  1.3 1.2 %copy-done = f32[256,1024]{1,0:T(8,128)S(1)} copy-done((f32[256,1024]{1,0:T(8,128)S(1)}, f32[256,1024]{1,0:T(8,128)}, u32[]{:S(2)}) %copy-start) | copy-done | bytes 1048600
  2.5 0.0 copy-start.1
  2.5 0.9 %copy-done.1 = f32[256,256]{1,0:T(8,128)S(1)} copy-done((f32[256,256]{1,0:T(8,128)S(1)}, f32[256,256]{1,0:T(8,128)}, u32[]{:S(2)}) %copy-start.1) | copy-done | bytes 262168
  3.5 0.0 copy-start.2
  3.5 0.9 %copy-done.2 = f32[8,24,256]{2,1,0:T(8,128)S(1)} copy-done((f32[8,24,256]{2,1,0:T(8,128)S(1)}, f32[8,24,256]{2,1,0:T(8,128)}, u32[]{:S(2)}) %copy-start.2) | copy-done | bytes 196632
  4.4 0.0 copy-start.3
  4.4 0.7 copy-done.3
  5.1 63.0 %gathered.1 = (f32[256,128]{1,0:T(8,128)S(1)}, f32[384,128]{1,0:T(8,128)S(1)}) custom-call(f32[256,1024]{1,0:T(8,128)S(1)} %copy-done, f32[8,24,256]{2,1,0:T(8,128)S(1)} %copy-done.2, f32[256,256]{1,0:T(8,128)S(1)} %copy-done.1, s32[8,128]{1,0:T(8,128)S(1)} %bitcast.1, f32[64]{0:T(128)S(1)} %copy-done.4), custom_call_target="tpu_custom_call" | custom-call | tf_op jit(solution)/shard_map/gathered/pallas_call | solution.py:267
  68.1 8.2 %factored.1 = (f32[128,256]{1,0:T(8,128)}, f32[256,256]{1,0:T(8,128)}) custom-call(f32[384,128]{1,0:T(8,128)S(1)} %get-tuple-element.4.cross, f32[256,128]{1,0:T(8,128)S(1)} %get-tuple-element.5.sketch), custom_call_target="tpu_custom_call" | custom-call | tf_op jit(solution)/shard_map/factored/pallas_call | solution.py:392
Async XLA Ops:
  0.6 0.7 copy-start.4
  1.3 1.2 %copy-start = (f32[256,1024]{1,0:T(8,128)S(1)}, f32[256,1024]{1,0:T(8,128)}, u32[]{:S(2)}) copy-start(f32[256,1024]{1,0:T(8,128)} %precip.1) | copy-start | bytes 3145732
  2.5 0.9 %copy-start.1 = (f32[256,256]{1,0:T(8,128)S(1)}, f32[256,256]{1,0:T(8,128)}, u32[]{:S(2)}) copy-start(f32[256,256]{1,0:T(8,128)} %test.1) | copy-start | bytes 786436
  3.5 0.9 %copy-start.2 = (f32[8,24,256]{2,1,0:T(8,128)S(1)}, f32[8,24,256]{2,1,0:T(8,128)}, u32[]{:S(2)}) copy-start(f32[8,24,256]{2,1,0:T(8,128)} %constant.2.clone.table) | copy-start | bytes 589828
  4.4 0.7 copy-start.3

commit v3 on v2

--- a/solution.py
+++ b/solution.py
@@ -37,16 +37,22 @@
 
 def gather_kernel(
     scale,
-    precip,
-    table,
-    test,
-    bins,
-    thresholds,
+    precip_hbm,
+    table_hbm,
+    test_hbm,
+    bins_hbm,
+    thresholds_hbm,
     sketch_out,
     cross_out,
     *scratch,
 ):
     (
+        precip,
+        table,
+        test,
+        bins,
+        thresholds,
+        load_sem,
         test_t,
         proj_out,
         proj_in,
@@ -77,6 +83,7 @@
     n_y, n_x, n_z = (lax.axis_size(a) for a in ("tm", "pts_0", "pts_1"))
     sends = []
 
+
     def send(src, dst, sem, device):
         copy = pltpu.make_async_remote_copy(
             src_ref=src,
@@ -102,7 +109,24 @@
     for other in others:
         pl.semaphore_signal(barrier, inc=1, device_id=other, device_id_type=MESH)
 
-    mine = table[y]
+    loads = [
+        pltpu.make_async_copy(src, dst, load_sem.at[i])
+        for i, (src, dst) in enumerate(
+            [
+                (table_hbm.at[y], table),
+                (precip_hbm, precip),
+                (test_hbm, test),
+                (bins_hbm, bins),
+                (thresholds_hbm, thresholds),
+            ]
+        )
+    ]
+    for copy in loads:
+        copy.start()
+
+    loads[0].wait()
+    loads[1].wait()
+    mine = table[...]
     proj = dot(mine, precip[...], ((1,), (0,)))
     for r in range(n_y):
         proj_out[r] = proj[:, 128 * r : 128 * (r + 1)]
@@ -110,6 +134,8 @@
     arrivals = []
     for o in [4, 3, 5, 2, 6, 1, 7]:
         arrivals.append(send(proj_out.at[y_at(o)], proj_in.at[o], proj_sem.at[o], {"tm": y_at(o)}))
+    for copy in loads[2:]:
+        copy.wait()
     test_t[...] = test[...].T
     found = bins[...]
     value = jnp.zeros(found.shape, jnp.float32)
@@ -259,20 +285,27 @@
 
 def gathered(precip, table, test, bins, thresholds, points_total):
     vmem = pl.BlockSpec(memory_space=pltpu.VMEM)
-    smem = pl.BlockSpec(memory_space=pltpu.SMEM)
+    hbm = pl.BlockSpec(memory_space=pltpu.HBM)
     f32 = jnp.float32
     dma = pltpu.SemaphoreType.DMA
     half = 192
     part = 24
+    operands = (precip, table, test, bins, thresholds)
     return pl.pallas_call(
         functools.partial(gather_kernel, 1.0 / points_total),
         out_shape=(
             jax.ShapeDtypeStruct((256, 128), f32),
             jax.ShapeDtypeStruct((384, 128), f32),
         ),
-        in_specs=[vmem, vmem, vmem, vmem, smem],
+        in_specs=[hbm] * 5,
         out_specs=(vmem, vmem),
         scratch_shapes=[
+            pltpu.VMEM(precip.shape, f32),
+            pltpu.VMEM(table.shape[1:], f32),
+            pltpu.VMEM(test.shape, f32),
+            pltpu.VMEM(bins.shape, jnp.int32),
+            pltpu.SMEM(thresholds.shape, f32),
+            dma((5,)),
             pltpu.VMEM((256, 256), f32),
             pltpu.VMEM((8, ROWS, 128), f32),
             pltpu.VMEM((8, ROWS, 128), f32),
@@ -300,7 +333,7 @@
             collective_id=0, has_side_effects=True, vmem_limit_bytes=40 << 20
         ),
         name="gathered",
-    )(precip, table, test, bins, thresholds)
+    )(*(pltpu.with_memory_space_constraint(a, pltpu.HBM) for a in operands))
 
 
 def terms(a):

time: 76.6 us -> 71.6 us (0.935)
  local copies, waits for them, and re-layouts: 4.43 us -> 0 us
    unnamed x10 -> x0, local copies, waits for them, and re-layouts: 4.43 us -> none
where the time goes in v3:
time: 71.6 us; the launch traced here: 71.4 us
  Pallas kernels  70.8 us (99%)
    pallas_call x1, Pallas kernels, gathered(): pl.pallas_call(functools.partial(gather_kernel, 1.0 / points_total), out_...  62.6 us
    pallas_call x1, Pallas kernels, factored(): pl.pallas_call(factor_kernel, out_shape=(jax.ShapeDtypeStruct((128, 256),...  8.21 us

profile of v3, /device:TPU:1, one launch (start us, length us, event | category | flops | bytes accessed | tf_op | source)
XLA Modules:
  0.0 71.4 jit_solution(12008788877388387042)
XLA Ops:
  0.6 62.6 %gathered.1 = (f32[256,128]{1,0:T(8,128)S(1)}, f32[384,128]{1,0:T(8,128)S(1)}) custom-call(f32[256,1024]{1,0:T(8,128)} %precip_hbm.1, f32[8,24,256]{2,1,0:T(8,128)} %constant.2.clone.table_hbm, f32[256,256]{1,0:T(8,128)} %test_hbm.1, s32[8,128]{1,0:T(8,128)} %bitcast.1, f32[64]{0:T(128)} %thresholds_hbm.1), custom_call_target="tpu_custom_call" | custom-call | tf_op jit(solution)/shard_map/gathered/pallas_call | solution.py:294
  63.2 8.2 %factored.1 = (f32[128,256]{1,0:T(8,128)}, f32[256,256]{1,0:T(8,128)}) custom-call(f32[384,128]{1,0:T(8,128)S(1)} %get-tuple-element.4.cross, f32[256,128]{1,0:T(8,128)S(1)} %get-tuple-element.5.sketch), custom_call_target="tpu_custom_call" | custom-call | tf_op jit(solution)/shard_map/factored/pallas_call | solution.py:425

commit v4 on v3

--- a/solution.py
+++ b/solution.py
@@ -16,7 +16,6 @@
 PTS = ("pts_0", "pts_1", "pts_2")
 PTS_TM = ("pts_0", "pts_1", "pts_2", "tm")
 MESH = pl.DeviceIdType.MESH
-HIGHEST = lax.Precision.HIGHEST
 
 
 def harmonic_basis(days):
@@ -29,10 +28,26 @@
     return np.linalg.solve(np.linalg.cholesky(table @ table.T), table)
 
 
-def dot(a, b, dims):
-    return lax.dot_general(
-        a, b, (dims, ((), ())), precision=HIGHEST, preferred_element_type=jnp.float32
-    )
+def terms(a):
+    first = a.astype(jnp.bfloat16)
+    rest = a - first.astype(jnp.float32)
+    second = rest.astype(jnp.bfloat16)
+    return first, second, (rest - second.astype(jnp.float32)).astype(jnp.bfloat16)
+
+
+LEFT, RIGHT = (0, 0, 1, 1, 0, 2), (0, 1, 0, 1, 2, 0)
+
+
+def left_of(parts, dim, count=6):
+    return jnp.concatenate([parts[i] for i in LEFT[:count]], dim)
+
+
+def right_of(parts, dim, count=6):
+    return jnp.concatenate([parts[i] for i in RIGHT[:count]], dim)
+
+
+def dot(a, b, dims=((1,), (0,))):
+    return lax.dot_general(a, b, (dims, ((), ())), preferred_element_type=jnp.float32)
 
 
 def gather_kernel(
@@ -54,6 +69,7 @@
         thresholds,
         load_sem,
         test_t,
+        table_t,
         proj_out,
         proj_in,
         coef,
@@ -126,17 +142,23 @@
 
     loads[0].wait()
     loads[1].wait()
-    mine = table[...]
-    proj = dot(mine, precip[...], ((1,), (0,)))
-    for r in range(n_y):
-        proj_out[r] = proj[:, 128 * r : 128 * (r + 1)]
+    one, two, three = terms(table[...])
+    stack = jnp.concatenate([one, two, three], 0)
+    for r in range(0, n_y, 2):
+        data = terms(precip[:, 128 * r : 128 * (r + 2)])
+        proj = dot(stack, data[0])
+        more = dot(stack[:64], data[1])
+        proj = proj[:32] + proj[32:64] + proj[64:] + more[:32] + more[32:] + dot(stack[:32], data[2])
+        proj_out[r] = proj[:ROWS, :128]
+        proj_out[r + 1] = proj[:ROWS, 128:]
     pl.semaphore_wait(barrier, len(others))
     arrivals = []
     for o in [4, 3, 5, 2, 6, 1, 7]:
         arrivals.append(send(proj_out.at[y_at(o)], proj_in.at[o], proj_sem.at[o], {"tm": y_at(o)}))
     for copy in loads[2:]:
         copy.wait()
-    test_t[...] = test[...].T
+    test_t[...] = left_of(terms(test[...].T), 1, TERMS)
+    table_t[...] = left_of((one, two, three), 0).T
     found = bins[...]
     value = jnp.zeros(found.shape, jnp.float32)
     for k in range(thresholds.shape[0]):
@@ -154,78 +176,64 @@
     for copy in arrivals:
         copy.wait_recv()
 
-    def partial(o):
-        r = y_at(o)
-        fit = dot(mine, coef[r], ((0,), (0,)))
-        data = precip[:, pl.ds(pl.multiple_of(128 * r, 128), 128)]
-        excess = jnp.maximum(data - fit - level[pl.ds(r, 1), :], 0.0)
-        sketch[o % n_y] = dot(test_t[...], excess, ((1,), (0,)))
-
-    n_p = ring.shape[1] // 2
-    piece = 128 // n_p
-
-    def chain(way, q, step):
-        hops = 4 if (q < n_p) == (way == 0) else 3
-        if step > hops:
-            return None
-        o = hops + 1 - step
-        return o if way == 0 else -o
-
-    def rows_of(q):
-        return pl.ds(q * piece, piece)
-
-    def hop(way, q, step):
-        o = chain(way, q, step) % n_y
-        src = sketch.at[o, rows_of(q)] if step == 1 else ring.at[way, q, step - 2]
-        return send(
-            src,
-            ring.at[way, q, step - 1],
-            ring_sem.at[way, q, step - 1],
-            {"tm": y_at(1 if way == 0 else -1)},
-        )
-
-    order = [(w, q) for q in range(n_p) for w in (0, 1)]
-    long = [(w, q if w == 0 else q + n_p) for w, q in order]
-    short = [(w, q + n_p if w == 0 else q) for w, q in order]
+    def partial(pair):
+        join = lambda f: jnp.concatenate([f(y_at(o)) for o in pair], 1)
+        found = join(lambda r: coef[r])
+        found = jnp.concatenate([found, jnp.zeros((32 - ROWS, found.shape[1]), jnp.float32)], 0)
+        fit = dot(table_t[...], right_of(terms(found), 0))
+        data = join(lambda r: precip[:, pl.ds(pl.multiple_of(128 * r, 128), 128)])
+        excess = jnp.maximum(data - fit - join(lambda r: level[pl.ds(r, 1), :]), 0.0)
+        sums = dot(test_t[...], right_of(terms(excess), 0, TERMS))
+        for i, o in enumerate(pair):
+            sketch[o % n_y] = sums[:, 128 * i : 128 * i + 128]
+
+    edges = [(h, s * a * t, s * b * t) for h, s in ((0, 1), (1, -1)) for side, t in ((LONG, -1), (SHORT, 1)) for a, b in side]
+    level_of = lambda e: max((1 + level_of(f) for f in edges if f[0] == e[0] and f[2] == e[1]), default=0)
+    edges.sort(key=lambda e: (level_of(e), -abs(e[1])))
+    piece = 128 // PIECES
     moving = {}
-    partial(4)
-    for w, q in long:
-        moving[w, q] = hop(w, q, 1)
-    partial(3)
-    for w, q in short:
-        if w == 0:
-            moving[w, q] = hop(w, q, 1)
-    partial(-3)
-    for w, q in short:
-        if w == 1:
-            moving[w, q] = hop(w, q, 1)
-    partial(2)
-    partial(-2)
-    for step in (2, 3, 4):
-        for w, q in long + short:
-            o = chain(w, q, step)
-            if o is None:
-                continue
-            moving[w, q].wait_recv()
-            ring[w, q, step - 2] += sketch[o % n_y, rows_of(q)]
-            moving[w, q] = hop(w, q, step)
-        if step == 2:
-            partial(1)
-            partial(-1)
-            partial(0)
-    for q in range(2 * n_p):
-        value = sketch[0, rows_of(q)]
-        for w in (0, 1):
-            hops = 4 if (w, q) in long else 3
-            moving[w, q].wait_recv()
-            value = value + ring[w, q, hops - 1]
-        sketch_out[rows_of(q)] = value
-
-    upper = sketch_out[:128]
-    lower = sketch_out[128:]
-    cross[:128] = dot(upper, upper, ((1,), (1,))) * scale
-    cross[128:256] = dot(upper, lower, ((1,), (1,))) * scale
-    cross[256:] = dot(lower, lower, ((1,), (1,))) * scale
+    ready = set()
+
+    def need(o):
+        for pair in PAIRS:
+            if o in [p % n_y for p in pair] and pair not in ready:
+                partial(pair)
+                ready.add(pair)
+
+    def arrived(h, a, q):
+        rows = pl.ds(128 * h + q * piece, piece)
+        value = sketch[-a % n_y, rows]
+        for i, e in enumerate(edges):
+            if e[0] == h and e[2] == a:
+                moving[i, q].wait_recv()
+                value = value + ring[i, pl.ds(q * piece, piece)]
+        return value
+
+    for i, (h, a, b) in enumerate(edges):
+        inner = [j for j, e in enumerate(edges) if e[0] == h and e[2] == a]
+        need(-a % n_y)
+        for q in range(PIECES):
+            if inner:
+                src = ring.at[inner[0], pl.ds(q * piece, piece)]
+                src[...] = arrived(h, a, q)
+            else:
+                src = sketch.at[-a % n_y, pl.ds(128 * h + q * piece, piece)]
+            moving[i, q] = send(
+                src, ring.at[i, pl.ds(q * piece, piece)], ring_sem.at[i, q], {"tm": y_at(b - a)}
+            )
+        if i == EARLY:
+            for o in range(n_y):
+                need(o)
+    for h in (0, 1):
+        for q in range(PIECES):
+            sketch_out[pl.ds(128 * h + q * piece, piece)] = arrived(h, 0, q)
+
+    parts = terms(sketch_out[...])
+    left = left_of(parts, 1)
+    right = right_of(parts, 1)
+    cross[:128] = dot(left[:128], right[:128], ((1,), (1,))) * scale
+    cross[128:256] = dot(left[:128], right[128:], ((1,), (1,))) * scale
+    cross[256:] = dot(left[128:], right[128:], ((1,), (1,))) * scale
     half = cross.shape[0] // 2
     part = half // n_y
     copy = send(
@@ -281,6 +289,11 @@
 
 
 PIECES = 2
+TERMS = 3
+PAIRS = ((4, 3), (-3, 2), (-2, 1), (-1, 0))
+EARLY = 5
+LONG = ((4, 2), (3, 2), (2, 1), (1, 0))
+SHORT = ((3, 2), (2, 1), (1, 0))
 
 
 def gathered(precip, table, test, bins, thresholds, points_total):
@@ -306,13 +319,14 @@
             pltpu.VMEM(bins.shape, jnp.int32),
             pltpu.SMEM(thresholds.shape, f32),
             dma((5,)),
-            pltpu.VMEM((256, 256), f32),
+            pltpu.VMEM((256, 256 * TERMS), jnp.bfloat16),
+            pltpu.VMEM((256, 192), jnp.bfloat16),
             pltpu.VMEM((8, ROWS, 128), f32),
             pltpu.VMEM((8, ROWS, 128), f32),
             pltpu.VMEM((8, ROWS, 128), f32),
             pltpu.VMEM((8, 128), f32),
             pltpu.VMEM((8, 256, 128), f32),
-            pltpu.VMEM((2, 2 * PIECES, 4, 128 // PIECES, 128), f32),
+            pltpu.VMEM((14, 128, 128), f32),
             pltpu.VMEM((384, 128), f32),
             pltpu.VMEM((half, 128), f32),
             pltpu.VMEM((8, part, 128), f32),
@@ -321,7 +335,7 @@
             pltpu.VMEM((384, 128), f32),
             dma((8, 2)),
             dma((8, 2)),
-            dma((2, 2 * PIECES, 4, 2)),
+            dma((14, PIECES, 2)),
             dma((2,)),
             dma((8, 2)),
             dma((8, 2)),
@@ -336,62 +350,62 @@
     )(*(pltpu.with_memory_space_constraint(a, pltpu.HBM) for a in operands))
 
 
-def terms(a):
-    first = a.astype(jnp.bfloat16)
-    rest = a - first.astype(jnp.float32)
-    second = rest.astype(jnp.bfloat16)
-    return first, second, (rest - second.astype(jnp.float32)).astype(jnp.bfloat16)
-
-
 BLOCK = 32
+STRIP = 16
 
 
 def factor_kernel(cross, sketch, basis_out, factor_out, work):
-    work[:128, :128] = cross[:128]
-    work[:128, 128:256] = cross[128:256]
-    work[128:, 128:256] = cross[256:]
-    work[:, 256:] = sketch[...]
     factor_out[128:, :128] = jnp.zeros((128, 128), jnp.float32)
     sub = lax.broadcasted_iota(jnp.int32, (8, 128), 0)
     lane = lax.broadcasted_iota(jnp.int32, (8, 128), 1)
     wide = lambda row: jnp.broadcast_to(row, (8, 128))
     groups = BLOCK // 8
+
+    def source(low, high, u):
+        if u == 2:
+            return sketch[low:high]
+        return cross[128 * u + low : 128 * u + high] if low < 128 else cross[128 + low : 128 + high]
+
     for first in range(0, 256, BLOCK):
         tile, start = first // 128, first % 128
         tiles = range(tile, 3)
-        rows = {
-            (g, u): work[first + 8 * g : first + 8 * g + 8, 128 * u : 128 * u + 128]
-            for g in range(groups)
-            for u in tiles
-        }
+        rows = {}
+        for g in range(groups):
+            low = first + 8 * g
+            for u in tiles:
+                rows[g, u] = (
+                    work[low : low + 8, 128 * u : 128 * u + 128] if first else source(low, low + 8, u)
+                )
+        root = {g: jnp.zeros((8, 128), jnp.float32) for g in range(groups)}
+        for open_at in range(0, BLOCK, STRIP):
+            strip = range(open_at, open_at + STRIP)
+            column = {
+                (j, h): wide(rows[h, tile][:, start + j : start + j + 1])
+                for j in strip
+                for h in range(j // 8, groups)
+            }
+            for j in strip:
+                g, i = divmod(j, 8)
+                pivot = wide(column[j, g][i : i + 1])
+                inverse = 1.0 / pivot
+                root[g] = jnp.where(sub == i, lax.rsqrt(pivot), root[g])
+                ratio = {h: column[j, h] * inverse for h in range(g, groups)}
+                for k in range(j + 1, strip.stop):
+                    value = wide(column[j, k // 8][k % 8 : k % 8 + 1])
+                    for h in range(k // 8, groups):
+                        column[k, h] = column[k, h] - ratio[h] * value
+                ratio[g] = jnp.where(sub > i, ratio[g], 0.0)
+                for u in tiles:
+                    row = wide(rows[g, u][i : i + 1])
+                    for h in range(g if i < 7 else g + 1, groups):
+                        rows[h, u] = rows[h, u] - ratio[h] * row
         done = {}
         for g in range(groups):
-            at = start + 8 * g
-            column = {
-                (j, h): wide(rows[h, tile][:, at + j : at + j + 1])
-                for j in range(8)
-                for h in range(g, groups)
-            }
-            root = jnp.zeros((8, 128), jnp.float32)
-            for j in range(8):
-                pivot = wide(column[j, g][j : j + 1])
-                inverse = 1.0 / pivot
-                root = jnp.where(sub == j, lax.rsqrt(pivot), root)
-                ratio = {h: column[j, h] * inverse for h in range(g, groups)}
-                for k in range(j + 1, 8):
-                    value = wide(column[j, g][k : k + 1])
-                    for h in range(g, groups):
-                        column[k, h] = column[k, h] - ratio[h] * value
-                ratio[g] = jnp.where(sub > j, ratio[g], 0.0)
-                for u in tiles:
-                    row = wide(rows[g, u][j : j + 1])
-                    for h in range(g if j < 7 else g + 1, groups):
-                        rows[h, u] = rows[h, u] - ratio[h] * row
             place = slice(first + 8 * g, first + 8 * g + 8)
             for u in tiles:
-                value = rows[g, u] * root
+                value = rows[g, u] * root[g]
                 if u == tile:
-                    value = jnp.where(lane >= at + sub, value, 0.0)
+                    value = jnp.where(lane >= start + 8 * g + sub, value, 0.0)
                 done[g, u] = value
                 if u < 2:
                     factor_out[place, 128 * u : 128 * u + 128] = value
@@ -404,17 +418,17 @@
         panel = jnp.concatenate(
             [jnp.concatenate([done[g, u] for u in tiles], 1) for g in range(groups)], 0
         )
-        one, two, three = terms(panel)
-        left = jnp.concatenate([one, one, two, two, one, three], 0)[:, : 256 - base].T
-        right = jnp.concatenate([one, two, one, two, three, one], 0)
+        parts = terms(panel)
+        left = left_of(parts, 0)[:, : 256 - base].T
+        right = right_of(parts, 0)
         ends = sorted({after, after + BLOCK, max(after, 128), 256})
         for low, high in zip(ends, ends[1:]):
             edge = 128 * (low // 128)
-            work[low:high, edge:] -= jnp.dot(
-                left[low - base : high - base],
-                right[:, edge - base :],
-                preferred_element_type=jnp.float32,
-            )
+            change = dot(left[low - base : high - base], right[:, edge - base :])
+            for u in range(edge // 128, 3):
+                old = work[low:high, 128 * u : 128 * u + 128] if first else source(low, high, u)
+                at = 128 * u - edge
+                work[low:high, 128 * u : 128 * u + 128] = old - change[:, at : at + 128]
     basis_out[:, :128] = work[:128, 256:].T
     basis_out[:, 128:] = work[128:, 256:].T
 
@@ -440,7 +454,7 @@
     days = precip.shape[0] * lax.axis_size("tm")
     points_total = precip.shape[1] * lax.axis_size(PTS)
     rows = harmonic_basis(days)
-    table = np.zeros((lax.axis_size("tm"), ROWS, precip.shape[0]), np.float32)
+    table = np.zeros((lax.axis_size("tm"), 32, precip.shape[0]), np.float32)
     table[:, : len(rows)] = rows.reshape(len(rows), -1, precip.shape[0]).swapaxes(0, 1)
     sketch_t, blocks = gathered(
         precip, table, test_matrix, bin_index.reshape(-1, 128), thresholds, points_total

time: 71.6 us -> 69.6 us (0.972)
  Pallas kernels: 70.8 us -> 68.9 us
    pallas_call x1, Pallas kernels: 8.21 us -> 6.73 us  [factored(): pl.pallas_call(factor_kernel, out_shape=(jax.ShapeDtypeStruct((128, 256),...]
where the time goes in v4:
time: 69.6 us; the launch traced here: 69.5 us
  Pallas kernels  68.9 us (99%)
    pallas_call x1, Pallas kernels, gathered(): pl.pallas_call(functools.partial(gather_kernel, 1.0 / points_total), out_...  62.1 us
    pallas_call x1, Pallas kernels, factored(): pl.pallas_call(factor_kernel, out_shape=(jax.ShapeDtypeStruct((128, 256),...  6.73 us

profile of v4, /device:TPU:1, one launch (start us, length us, event | category | flops | bytes accessed | tf_op | source)
XLA Modules:
  0.0 69.5 jit_solution(4569501204117504298)
XLA Ops:
  0.6 62.1 %gathered.1 = (f32[256,128]{1,0:T(8,128)S(1)}, f32[384,128]{1,0:T(8,128)S(1)}) custom-call(f32[256,1024]{1,0:T(8,128)} %precip_hbm.1, f32[8,32,256]{2,1,0:T(8,128)} %constant.2.clone.table_hbm, f32[256,256]{1,0:T(8,128)} %test_hbm.1, s32[8,128]{1,0:T(8,128)} %bitcast.1, f32[64]{0:T(128)} %thresholds_hbm.1), custom_call_target="tpu_custom_call" | custom-call | tf_op jit(solution)/shard_map/gathered/pallas_call | solution.py:307
  62.8 6.7 %factored.1 = (f32[128,256]{1,0:T(8,128)}, f32[256,256]{1,0:T(8,128)}) custom-call(f32[384,128]{1,0:T(8,128)S(1)} %get-tuple-element.4.cross, f32[256,128]{1,0:T(8,128)S(1)} %get-tuple-element.5.sketch), custom_call_target="tpu_custom_call" | custom-call | tf_op jit(solution)/shard_map/factored/pallas_call | solution.py:439

commit v5 on v4

--- a/solution.py
+++ b/solution.py
@@ -12,7 +12,7 @@
 
 HARM = 8
 YEAR_DAYS = 365.25
-ROWS = 24
+ROWS = 2 * HARM + 1
 PTS = ("pts_0", "pts_1", "pts_2")
 PTS_TM = ("pts_0", "pts_1", "pts_2", "tm")
 MESH = pl.DeviceIdType.MESH
@@ -117,6 +117,7 @@
     x_at = lambda o: lax.rem(x + o + n_x, n_x)
     z_at = lambda o: lax.rem(z + o + n_z, n_z)
 
+    coef[:, 16:] = jnp.zeros((n_y, 16, 128), jnp.float32)
     barrier = pltpu.get_barrier_semaphore()
     others = [{"tm": y_at(o)} for o in range(1, n_y)]
     others += [{"pts_0": x_at(o)} for o in range(1, n_x)]
@@ -169,17 +170,17 @@
     own = proj_out[y]
     for o in range(1, n_y):
         own = own + proj_in[o]
-    coef[y] = own
+    coef[y, :ROWS] = own
+    mine = coef.at[y, pl.ds(0, ROWS)]
     arrivals = []
     for o in [4, 3, 5, 2, 6, 1, 7]:
-        arrivals.append(send(coef.at[y], coef.at[y], coef_sem.at[o], {"tm": y_at(o)}))
+        arrivals.append(send(mine, mine, coef_sem.at[o], {"tm": y_at(o)}))
     for copy in arrivals:
         copy.wait_recv()
 
     def partial(pair):
         join = lambda f: jnp.concatenate([f(y_at(o)) for o in pair], 1)
         found = join(lambda r: coef[r])
-        found = jnp.concatenate([found, jnp.zeros((32 - ROWS, found.shape[1]), jnp.float32)], 0)
         fit = dot(table_t[...], right_of(terms(found), 0))
         data = join(lambda r: precip[:, pl.ds(pl.multiple_of(128 * r, 128), 128)])
         excess = jnp.maximum(data - fit - join(lambda r: level[pl.ds(r, 1), :]), 0.0)
@@ -231,29 +232,24 @@
     parts = terms(sketch_out[...])
     left = left_of(parts, 1)
     right = right_of(parts, 1)
-    cross[:128] = dot(left[:128], right[:128], ((1,), (1,))) * scale
-    cross[128:256] = dot(left[:128], right[128:], ((1,), (1,))) * scale
-    cross[256:] = dot(left[128:], right[128:], ((1,), (1,))) * scale
-    half = cross.shape[0] // 2
-    part = half // n_y
-    copy = send(
-        cross.at[pl.ds(pl.multiple_of((1 - c) * half, 8), half)], core_in, core_sem, {"pts_2": 1 - c}
-    )
+    first = dot(left[:128], right[:128], ((1,), (1,))) * scale
+    mixed = dot(left[:128], right[128:], ((1,), (1,))) * scale
+    second = dot(left[128:], right[128:], ((1,), (1,))) * scale
+    row = lax.broadcasted_iota(jnp.int32, (128, 128), 0)
+    lane = lax.broadcasted_iota(jnp.int32, (128, 128), 1)
+    cross[0, :, :16] = mixed.reshape(n_y, 16, 128)
+    cross[1, :, :16] = jnp.where(row <= lane, first, second).reshape(n_y, 16, 128)
+    cross[:, :, 16:] = jnp.zeros((2, n_y, 1, 128), jnp.float32)
+    cross[1, 0, 16:] = jnp.sum(jnp.where(row == lane, second, 0.0), axis=0, keepdims=True)
+    copy = send(cross.at[1 - c], core_in, core_sem, {"pts_2": 1 - c})
     copy.wait_recv()
-    core_in[...] += cross[pl.ds(pl.multiple_of(c * half, 8), half)]
+    core_in[...] += cross[c]
     arrivals = []
     for o in [4, 3, 5, 2, 6, 1, 7]:
-        arrivals.append(
-            send(
-                core_in.at[pl.ds(pl.multiple_of(y_at(o) * part, 8), part)],
-                y_in.at[o],
-                y_sem.at[o],
-                {"tm": y_at(o)},
-            )
-        )
-    for copy in arrivals:
-        copy.wait_recv()
-    own = core_in[pl.ds(pl.multiple_of(y * part, 8), part)]
+        arrivals.append(send(core_in.at[y_at(o)], y_in.at[o], y_sem.at[o], {"tm": y_at(o)}))
+    for copy in arrivals:
+        copy.wait_recv()
+    own = core_in[y]
     for o in range(1, n_y):
         own = own + y_in[o]
     z_in[z] = own
@@ -274,16 +270,20 @@
     own = x_in[0]
     for o in range(1, n_x):
         own = own + x_in[o]
-    place = pl.ds(pl.multiple_of(c * half + y * part, 8), part)
-    total[place] = own
+    total[c, y] = own
+    place = total.at[c, y]
     arrivals = []
     for o in [4, 3, 5, 2, 6, 1, 7]:
-        arrivals.append(send(total.at[place], total.at[place], gather_sem.at[o], {"tm": y_at(o)}))
-    for copy in arrivals:
-        copy.wait_recv()
-    place = pl.ds(pl.multiple_of(c * half, 8), half)
-    send(total.at[place], total.at[place], join_sem, {"pts_2": 1 - c}).wait_recv()
-    cross_out[...] = total[...]
+        arrivals.append(send(place, place, gather_sem.at[o], {"tm": y_at(o)}))
+    for copy in arrivals:
+        copy.wait_recv()
+    place = total.at[c]
+    send(place, place, join_sem, {"pts_2": 1 - c}).wait_recv()
+    both = total[1, :, :16].reshape(128, 128)
+    turned = both.T
+    cross_out[:128] = jnp.where(row <= lane, both, turned)
+    cross_out[128:256] = total[0, :, :16].reshape(128, 128)
+    cross_out[256:] = jnp.where(row == lane, total[1, 0, 16:], jnp.where(row > lane, both, turned))
     for copy in sends:
         copy.wait_send()
 
@@ -301,8 +301,6 @@
     hbm = pl.BlockSpec(memory_space=pltpu.HBM)
     f32 = jnp.float32
     dma = pltpu.SemaphoreType.DMA
-    half = 192
-    part = 24
     operands = (precip, table, test, bins, thresholds)
     return pl.pallas_call(
         functools.partial(gather_kernel, 1.0 / points_total),
@@ -323,16 +321,16 @@
             pltpu.VMEM((256, 192), jnp.bfloat16),
             pltpu.VMEM((8, ROWS, 128), f32),
             pltpu.VMEM((8, ROWS, 128), f32),
-            pltpu.VMEM((8, ROWS, 128), f32),
+            pltpu.VMEM((8, 32, 128), f32),
             pltpu.VMEM((8, 128), f32),
             pltpu.VMEM((8, 256, 128), f32),
             pltpu.VMEM((14, 128, 128), f32),
-            pltpu.VMEM((384, 128), f32),
-            pltpu.VMEM((half, 128), f32),
-            pltpu.VMEM((8, part, 128), f32),
-            pltpu.VMEM((8, part, 128), f32),
-            pltpu.VMEM((4, part, 128), f32),
-            pltpu.VMEM((384, 128), f32),
+            pltpu.VMEM((2, 8, 17, 128), f32),
+            pltpu.VMEM((8, 17, 128), f32),
+            pltpu.VMEM((8, 17, 128), f32),
+            pltpu.VMEM((8, 17, 128), f32),
+            pltpu.VMEM((4, 17, 128), f32),
+            pltpu.VMEM((2, 8, 17, 128), f32),
             dma((8, 2)),
             dma((8, 2)),
             dma((14, PIECES, 2)),

time: 69.6 us -> 68.6 us (0.986)
  Pallas kernels: 68.9 us -> 67.8 us
    pallas_call x1, Pallas kernels: 62.1 us -> 61.1 us  [gathered(): pl.pallas_call(functools.partial(gather_kernel, 1.0 / points_total), out_...]
where the time goes in v5:
time: 68.6 us; the launch traced here: 68.5 us
  Pallas kernels  67.8 us (99%)
    pallas_call x1, Pallas kernels, gathered(): pl.pallas_call(functools.partial(gather_kernel, 1.0 / points_total), out_...  61.1 us
    pallas_call x1, Pallas kernels, factored(): pl.pallas_call(factor_kernel, out_shape=(jax.ShapeDtypeStruct((128, 256),...  6.73 us

profile of v5, /device:TPU:1, one launch (start us, length us, event | category | flops | bytes accessed | tf_op | source)
XLA Modules:
  0.0 68.5 jit_solution(3707824627025422943)
XLA Ops:
  0.6 61.1 %gathered.1 = (f32[256,128]{1,0:T(8,128)S(1)}, f32[384,128]{1,0:T(8,128)S(1)}) custom-call(f32[256,1024]{1,0:T(8,128)} %precip_hbm.1, f32[8,32,256]{2,1,0:T(8,128)} %constant.2.clone.table_hbm, f32[256,256]{1,0:T(8,128)} %test_hbm.1, s32[8,128]{1,0:T(8,128)} %bitcast.1, f32[64]{0:T(128)} %thresholds_hbm.1), custom_call_target="tpu_custom_call" | custom-call | tf_op jit(solution)/shard_map/gathered/pallas_call | solution.py:305
  61.8 6.7 %factored.1 = (f32[128,256]{1,0:T(8,128)}, f32[256,256]{1,0:T(8,128)}) custom-call(f32[384,128]{1,0:T(8,128)S(1)} %get-tuple-element.4.cross, f32[256,128]{1,0:T(8,128)S(1)} %get-tuple-element.5.sketch), custom_call_target="tpu_custom_call" | custom-call | tf_op jit(solution)/shard_map/factored/pallas_call | solution.py:437

commit v6 on v5

--- a/solution.py
+++ b/solution.py
@@ -99,7 +99,6 @@
     n_y, n_x, n_z = (lax.axis_size(a) for a in ("tm", "pts_0", "pts_1"))
     sends = []
 
-
     def send(src, dst, sem, device):
         copy = pltpu.make_async_remote_copy(
             src_ref=src,
@@ -119,9 +118,9 @@
 
     coef[:, 16:] = jnp.zeros((n_y, 16, 128), jnp.float32)
     barrier = pltpu.get_barrier_semaphore()
-    others = [{"tm": y_at(o)} for o in range(1, n_y)]
+    others = [{"tm": y_at(o)} for o in FAR]
     others += [{"pts_0": x_at(o)} for o in range(1, n_x)]
-    others += [{"pts_1": z_at(o)} for o in range(1, n_z)]
+    others += [{"pts_1": z_at(o)} for o in FAR]
     others += [{"pts_2": 1 - c}]
     for other in others:
         pl.semaphore_signal(barrier, inc=1, device_id=other, device_id_type=MESH)
@@ -154,7 +153,7 @@
         proj_out[r + 1] = proj[:ROWS, 128:]
     pl.semaphore_wait(barrier, len(others))
     arrivals = []
-    for o in [4, 3, 5, 2, 6, 1, 7]:
+    for o in FAR:
         arrivals.append(send(proj_out.at[y_at(o)], proj_in.at[o], proj_sem.at[o], {"tm": y_at(o)}))
     for copy in loads[2:]:
         copy.wait()
@@ -173,7 +172,7 @@
     coef[y, :ROWS] = own
     mine = coef.at[y, pl.ds(0, ROWS)]
     arrivals = []
-    for o in [4, 3, 5, 2, 6, 1, 7]:
+    for o in FAR:
         arrivals.append(send(mine, mine, coef_sem.at[o], {"tm": y_at(o)}))
     for copy in arrivals:
         copy.wait_recv()
@@ -193,13 +192,8 @@
     edges.sort(key=lambda e: (level_of(e), -abs(e[1])))
     piece = 128 // PIECES
     moving = {}
-    ready = set()
-
-    def need(o):
-        for pair in PAIRS:
-            if o in [p % n_y for p in pair] and pair not in ready:
-                partial(pair)
-                ready.add(pair)
+
+    partial(FIRST)
 
     def arrived(h, a, q):
         rows = pl.ds(128 * h + q * piece, piece)
@@ -212,7 +206,9 @@
 
     for i, (h, a, b) in enumerate(edges):
         inner = [j for j, e in enumerate(edges) if e[0] == h and e[2] == a]
-        need(-a % n_y)
+        if i == sum(level_of(e) == 0 for e in edges):
+            for chunks in LATER:
+                partial(chunks)
         for q in range(PIECES):
             if inner:
                 src = ring.at[inner[0], pl.ds(q * piece, piece)]
@@ -222,9 +218,6 @@
             moving[i, q] = send(
                 src, ring.at[i, pl.ds(q * piece, piece)], ring_sem.at[i, q], {"tm": y_at(b - a)}
             )
-        if i == EARLY:
-            for o in range(n_y):
-                need(o)
     for h in (0, 1):
         for q in range(PIECES):
             sketch_out[pl.ds(128 * h + q * piece, piece)] = arrived(h, 0, q)
@@ -245,7 +238,7 @@
     copy.wait_recv()
     core_in[...] += cross[c]
     arrivals = []
-    for o in [4, 3, 5, 2, 6, 1, 7]:
+    for o in FAR:
         arrivals.append(send(core_in.at[y_at(o)], y_in.at[o], y_sem.at[o], {"tm": y_at(o)}))
     for copy in arrivals:
         copy.wait_recv()
@@ -254,7 +247,7 @@
         own = own + y_in[o]
     z_in[z] = own
     arrivals = []
-    for o in [4, 3, 5, 2, 6, 1, 7]:
+    for o in FAR:
         arrivals.append(send(z_in.at[z], z_in.at[z], z_sem.at[o], {"pts_1": z_at(o)}))
     for copy in arrivals:
         copy.wait_recv()
@@ -273,7 +266,7 @@
     total[c, y] = own
     place = total.at[c, y]
     arrivals = []
-    for o in [4, 3, 5, 2, 6, 1, 7]:
+    for o in FAR:
         arrivals.append(send(place, place, gather_sem.at[o], {"tm": y_at(o)}))
     for copy in arrivals:
         copy.wait_recv()
@@ -288,10 +281,11 @@
         copy.wait_send()
 
 
+FAR = (4, 3, 5, 2, 6, 1, 7)
 PIECES = 2
 TERMS = 3
-PAIRS = ((4, 3), (-3, 2), (-2, 1), (-1, 0))
-EARLY = 5
+FIRST = (4, 3, -3)
+LATER = ((2, -2), (1, -1), (0,))
 LONG = ((4, 2), (3, 2), (2, 1), (1, 0))
 SHORT = ((3, 2), (2, 1), (1, 0))
 

time: 68.6 us -> 68.6 us (level)
  no operation moved by 1% of the time
where the time goes in v6:
time: 68.6 us; the launch traced here: 68.5 us
  Pallas kernels  67.8 us (99%)
    pallas_call x1, Pallas kernels, gathered(): pl.pallas_call(functools.partial(gather_kernel, 1.0 / points_total), out_...  61.1 us
    pallas_call x1, Pallas kernels, factored(): pl.pallas_call(factor_kernel, out_shape=(jax.ShapeDtypeStruct((128, 256),...  6.72 us

profile of v6, /device:TPU:1, one launch (start us, length us, event | category | flops | bytes accessed | tf_op | source)
XLA Modules:
  0.0 68.5 jit_solution(8686375933538456859)
XLA Ops:
  0.6 61.1 %gathered.1 = (f32[256,128]{1,0:T(8,128)S(1)}, f32[384,128]{1,0:T(8,128)S(1)}) custom-call(f32[256,1024]{1,0:T(8,128)} %precip_hbm.1, f32[8,32,256]{2,1,0:T(8,128)} %constant.2.clone.table_hbm, f32[256,256]{1,0:T(8,128)} %test_hbm.1, s32[8,128]{1,0:T(8,128)} %bitcast.1, f32[64]{0:T(128)} %thresholds_hbm.1), custom_call_target="tpu_custom_call" | custom-call | tf_op jit(solution)/shard_map/gathered/pallas_call | solution.py:299
  61.7 6.7 %factored.1 = (f32[128,256]{1,0:T(8,128)}, f32[256,256]{1,0:T(8,128)}) custom-call(f32[384,128]{1,0:T(8,128)S(1)} %get-tuple-element.4.cross, f32[256,128]{1,0:T(8,128)S(1)} %get-tuple-element.5.sketch), custom_call_target="tpu_custom_call" | custom-call | tf_op jit(solution)/shard_map/factored/pallas_call | solution.py:431

commit v7 on v6

--- a/solution.py
+++ b/solution.py
@@ -234,11 +234,16 @@
     cross[1, :, :16] = jnp.where(row <= lane, first, second).reshape(n_y, 16, 128)
     cross[:, :, 16:] = jnp.zeros((2, n_y, 1, 128), jnp.float32)
     cross[1, 0, 16:] = jnp.sum(jnp.where(row == lane, second, 0.0), axis=0, keepdims=True)
-    copy = send(cross.at[1 - c], core_in, core_sem, {"pts_2": 1 - c})
-    copy.wait_recv()
-    core_in[...] += cross[c]
+    halves = {}
+    for o in (*FAR, 0):
+        r = y_at(o)
+        halves[o] = send(cross.at[1 - c, r], core_in.at[r], core_sem.at[o], {"pts_2": 1 - c})
     arrivals = []
-    for o in FAR:
+    for o in (*FAR, 0):
+        halves[o].wait_recv()
+        core_in[y_at(o)] += cross[c, y_at(o)]
+        if o == 0:
+            continue
         arrivals.append(send(core_in.at[y_at(o)], y_in.at[o], y_sem.at[o], {"tm": y_at(o)}))
     for copy in arrivals:
         copy.wait_recv()
@@ -265,13 +270,16 @@
         own = own + x_in[o]
     total[c, y] = own
     place = total.at[c, y]
-    arrivals = []
+    arrivals = {}
     for o in FAR:
-        arrivals.append(send(place, place, gather_sem.at[o], {"tm": y_at(o)}))
-    for copy in arrivals:
-        copy.wait_recv()
-    place = total.at[c]
-    send(place, place, join_sem, {"pts_2": 1 - c}).wait_recv()
+        arrivals[o] = send(place, place, gather_sem.at[o], {"tm": y_at(o)})
+    joins = [send(place, place, join_sem.at[0], {"pts_2": 1 - c})]
+    for o in (1, 7, 2, 6, 3, 5, 4):
+        arrivals[o].wait_recv()
+        place = total.at[c, y_at(-o)]
+        joins.append(send(place, place, join_sem.at[o], {"pts_2": 1 - c}))
+    for copy in joins:
+        copy.wait_recv()
     both = total[1, :, :16].reshape(128, 128)
     turned = both.T
     cross_out[:128] = jnp.where(row <= lane, both, turned)
@@ -328,12 +336,12 @@
             dma((8, 2)),
             dma((8, 2)),
             dma((14, PIECES, 2)),
-            dma((2,)),
+            dma((8, 2)),
             dma((8, 2)),
             dma((8, 2)),
             dma((4, 2)),
             dma((8, 2)),
-            dma((2,)),
+            dma((8, 2)),
         ],
         compiler_params=pltpu.CompilerParams(
             collective_id=0, has_side_effects=True, vmem_limit_bytes=40 << 20

time: 68.6 us -> 68.8 us (level)
  no operation moved by 1% of the time
where the time goes in v7:
time: 68.8 us; the launch traced here: 68.7 us
  Pallas kernels  68 us (99%)
    pallas_call x1, Pallas kernels, gathered(): pl.pallas_call(functools.partial(gather_kernel, 1.0 / points_total), out_...  61.3 us
    pallas_call x1, Pallas kernels, factored(): pl.pallas_call(factor_kernel, out_shape=(jax.ShapeDtypeStruct((128, 256),...  6.73 us

profile of v7, /device:TPU:1, one launch (start us, length us, event | category | flops | bytes accessed | tf_op | source)
XLA Modules:
  0.0 68.7 jit_solution(1173066778320230740)
XLA Ops:
  0.6 61.3 %gathered.1 = (f32[256,128]{1,0:T(8,128)S(1)}, f32[384,128]{1,0:T(8,128)S(1)}) custom-call(f32[256,1024]{1,0:T(8,128)} %precip_hbm.1, f32[8,32,256]{2,1,0:T(8,128)} %constant.2.clone.table_hbm, f32[256,256]{1,0:T(8,128)} %test_hbm.1, s32[8,128]{1,0:T(8,128)} %bitcast.1, f32[64]{0:T(128)} %thresholds_hbm.1), custom_call_target="tpu_custom_call" | custom-call | tf_op jit(solution)/shard_map/gathered/pallas_call | solution.py:307
  61.9 6.7 %factored.1 = (f32[128,256]{1,0:T(8,128)}, f32[256,256]{1,0:T(8,128)}) custom-call(f32[384,128]{1,0:T(8,128)S(1)} %get-tuple-element.4.cross, f32[256,128]{1,0:T(8,128)S(1)} %get-tuple-element.5.sketch), custom_call_target="tpu_custom_call" | custom-call | tf_op jit(solution)/shard_map/factored/pallas_call | solution.py:439

commit v8 on v6

--- a/solution.py
+++ b/solution.py
@@ -153,6 +153,8 @@
         proj_out[r + 1] = proj[:ROWS, 128:]
     pl.semaphore_wait(barrier, len(others))
     arrivals = []
+    due = sends[:]
+    sends.clear()
     for o in FAR:
         arrivals.append(send(proj_out.at[y_at(o)], proj_in.at[o], proj_sem.at[o], {"tm": y_at(o)}))
     for copy in loads[2:]:
@@ -164,6 +166,8 @@
     for k in range(thresholds.shape[0]):
         value = jnp.where(found == k, thresholds[k], value)
     level[...] = value
+    for copy in due:
+        copy.wait_send()
     for copy in arrivals:
         copy.wait_recv()
     own = proj_out[y]
@@ -172,8 +176,12 @@
     coef[y, :ROWS] = own
     mine = coef.at[y, pl.ds(0, ROWS)]
     arrivals = []
+    due = sends[:]
+    sends.clear()
     for o in FAR:
         arrivals.append(send(mine, mine, coef_sem.at[o], {"tm": y_at(o)}))
+    for copy in due:
+        copy.wait_send()
     for copy in arrivals:
         copy.wait_recv()
 
@@ -238,8 +246,12 @@
     copy.wait_recv()
     core_in[...] += cross[c]
     arrivals = []
+    due = sends[:]
+    sends.clear()
     for o in FAR:
         arrivals.append(send(core_in.at[y_at(o)], y_in.at[o], y_sem.at[o], {"tm": y_at(o)}))
+    for copy in due:
+        copy.wait_send()
     for copy in arrivals:
         copy.wait_recv()
     own = core_in[y]
@@ -247,8 +259,12 @@
         own = own + y_in[o]
     z_in[z] = own
     arrivals = []
+    due = sends[:]
+    sends.clear()
     for o in FAR:
         arrivals.append(send(z_in.at[z], z_in.at[z], z_sem.at[o], {"pts_1": z_at(o)}))
+    for copy in due:
+        copy.wait_send()
     for copy in arrivals:
         copy.wait_recv()
     own = z_in[0]
@@ -256,8 +272,12 @@
         own = own + z_in[o]
     x_in[x] = own
     arrivals = []
+    due = sends[:]
+    sends.clear()
     for o in [2, 1, 3]:
         arrivals.append(send(x_in.at[x], x_in.at[x], x_sem.at[o], {"pts_0": x_at(o)}))
+    for copy in due:
+        copy.wait_send()
     for copy in arrivals:
         copy.wait_recv()
     own = x_in[0]
@@ -266,8 +286,12 @@
     total[c, y] = own
     place = total.at[c, y]
     arrivals = []
+    due = sends[:]
+    sends.clear()
     for o in FAR:
         arrivals.append(send(place, place, gather_sem.at[o], {"tm": y_at(o)}))
+    for copy in due:
+        copy.wait_send()
     for copy in arrivals:
         copy.wait_recv()
     place = total.at[c]

time: 68.6 us -> 68.5 us (level)
  no operation moved by 1% of the time
where the time goes in v8:
time: 68.5 us; the launch traced here: 68.4 us
  Pallas kernels  67.7 us (99%)
    pallas_call x1, Pallas kernels, gathered(): pl.pallas_call(functools.partial(gather_kernel, 1.0 / points_total), out_...  61 us
    pallas_call x1, Pallas kernels, factored(): pl.pallas_call(factor_kernel, out_shape=(jax.ShapeDtypeStruct((128, 256),...  6.73 us

profile of v8, /device:TPU:1, one launch (start us, length us, event | category | flops | bytes accessed | tf_op | source)
XLA Modules:
  0.0 68.4 jit_solution(16155646627193136060)
XLA Ops:
  0.6 61.0 %gathered.1 = (f32[256,128]{1,0:T(8,128)S(1)}, f32[384,128]{1,0:T(8,128)S(1)}) custom-call(f32[256,1024]{1,0:T(8,128)} %precip_hbm.1, f32[8,32,256]{2,1,0:T(8,128)} %constant.2.clone.table_hbm, f32[256,256]{1,0:T(8,128)} %test_hbm.1, s32[8,128]{1,0:T(8,128)} %bitcast.1, f32[64]{0:T(128)} %thresholds_hbm.1), custom_call_target="tpu_custom_call" | custom-call | tf_op jit(solution)/shard_map/gathered/pallas_call | solution.py:323
  61.6 6.7 %factored.1 = (f32[128,256]{1,0:T(8,128)}, f32[256,256]{1,0:T(8,128)}) custom-call(f32[384,128]{1,0:T(8,128)S(1)} %get-tuple-element.4.cross, f32[256,128]{1,0:T(8,128)S(1)} %get-tuple-element.5.sketch), custom_call_target="tpu_custom_call" | custom-call | tf_op jit(solution)/shard_map/factored/pallas_call | solution.py:455
